TPU v7x, 32 devices: a whole 2x2x4 slice. The times are simulated.
32 devices in a mesh: section: 4 (over y, x), elem: 8 (over z, core).
Axes of the slice: x: 2, y: 2, z: 4, core: 2. Of those that a mesh axis runs over, the one named last changes fastest.
Arguments:
- interior_res: bfloat16 [3, 8, 4, 48, 100], P(None, 'elem', 'section'), may hold values from -1.5 to 1.5
- face_res: bfloat16 [3, 8, 4, 48, 4, 50], P(None, 'elem', 'section'), may hold values from -1.5 to 1.5
- trace_vals: bfloat16 [3, 8, 4, 48, 4, 50], P(None, 'elem', 'section'), may hold values from -1.5 to 1.5
- stabil: bfloat16 [8, 4, 48, 4, 25], P('elem'), may hold values from -2.5 to 2.5
- element_faces: int32 [8, 4, 48, 4], P('elem'), may hold values from 0 to 3071, as said below
- orient: int32 [8, 4, 48, 4, 10], P('elem'), may hold values from 0 to 9, as said below
- lift_matrix: bfloat16 [4, 20, 10], replicated, may hold values from -2 to 2
- face_matrix: bfloat16 [10, 10], replicated, may hold values from -2 to 2
- factors: bfloat16 [4, 8, 100, 19200], P('section', 'elem'), may hold values from -0.625 to 0.625
Outputs:
- trace_residual: float32 [3, 3072, 50], P(None, ('section', 'elem'))
- schur_product: float32 [3, 3072, 50], P(None, ('section', 'elem'))
Inputs may be any that keep to these rules, and one draw needn't show every extreme that they name: `element_faces`: every face number is named by exactly two element faces. Face f is owned by column (f // 96) % 8. For every other column, exactly 2 of a column's element faces name faces owned by that column; the rest name faces owned by the column itself. `orient`: each row of 10 numbers is one of the six node orders that the symmetries of a triangle give to the ten nodes of its degree-3 lattice.
All inputs are finite; a program needn't handle non-finite values.
Results may differ from a plain program's by a relative error of at most 0.004.
Values may be sent and summed in bfloat16 or wider, within the bound.
A program may use at most 128 MiB of HBM per device.

v0:
```python
import jax
import jax.numpy as jnp
from jax import lax
from jax.sharding import PartitionSpec as P

radau_inverse = (
    (4.325579890063155, 0.33919925181580984, 0.5417705399358749),
    (-4.178718591551905, -0.32768282076106237, 0.47662355450055044),
    (-0.5028726349457868, 2.571926949855605, -0.5960392048282249),
)


def transform(sections):
    values = sections.astype(jnp.float32)
    return jnp.stack(
        [
            radau_inverse[row_index][0] * values[0]
            + radau_inverse[row_index][1] * values[1]
            + radau_inverse[row_index][2] * values[2]
            for row_index in range(3)
        ]
    ).astype(jnp.bfloat16)


def condense(
    inner_part, face_part, trace_part, stab_block, lift_matrix, face_matrix, apply_inverse
):
    highest = lax.Precision.HIGHEST
    components = inner_part.shape[0]
    number = inner_part.shape[1]
    var_count = stab_block.shape[-1]
    mode_count = inner_part.shape[2] // var_count
    lift_wide = lift_matrix.astype(jnp.float32)
    weighted = jnp.einsum(
        "ekvu,ceknu->ceknv", stab_block, trace_part, preferred_element_type=jnp.float32
    )
    lifted = jnp.einsum("kmn,ceknv->cemv", lift_wide, weighted, precision=highest)
    lifted = lifted.reshape(components, number, mode_count * var_count).astype(jnp.bfloat16)
    solved = apply_inverse(jnp.stack([inner_part, lifted], 1))
    shaped = solved.reshape(components, 2, number, mode_count, var_count)
    weighted_solve = jnp.einsum(
        "ekvu,cremu->crekmv", stab_block.astype(jnp.float32), shaped, precision=highest
    )
    coupled = jnp.einsum("kmn,crekmv->creknv", lift_wide, weighted_solve, precision=highest)
    face_term = jnp.einsum(
        "nj,cekjv->ceknv", face_matrix.astype(jnp.float32), weighted, precision=highest
    )
    return jnp.stack([face_part.astype(jnp.float32) - coupled[:, 0], face_term - coupled[:, 1]], 1)


def on_device(
    interior_res,
    face_res,
    trace_vals,
    stabil,
    element_faces,
    orient,
    lift_matrix,
    face_matrix,
    factors,
):
    elem_count = interior_res.shape[3]
    inner_size = interior_res.shape[4]
    face_size = face_res.shape[5]
    fnodes = face_matrix.shape[0]
    var_count = face_size // fnodes
    columns = lax.axis_size("elem")
    col_elems = 4 * elem_count
    third_count = elem_count // 3
    group_elems = 4 * third_count
    share_slots = elem_count // 24
    face_dev = 2 * elem_count
    col_faces = 4 * face_dev
    row_width = inner_size + 8 * face_size
    payload_width = 6 * face_size
    packed = jnp.concatenate(
        [
            interior_res.reshape(3, elem_count, inner_size),
            face_res.reshape(3, elem_count, 4 * face_size),
            trace_vals.reshape(3, elem_count, 4 * face_size),
        ],
        axis=2,
    )
    section_w = transform(packed)
    real_slot = section_w[0].reshape(1, elem_count * row_width)
    complex_slot = section_w[1:3].reshape(2, third_count, 3, row_width).transpose(2, 0, 1, 3)
    complex_slot = complex_slot.reshape(3, 2 * third_count * row_width)
    padding = jnp.zeros((3, elem_count * row_width - 2 * third_count * row_width), jnp.bfloat16)
    outgoing = jnp.concatenate(
        [real_slot, jnp.concatenate([complex_slot, padding], axis=1)], axis=0
    )
    received = lax.all_to_all(outgoing, "section", split_axis=0, concat_axis=0, tiled=True)
    section_index = lax.axis_index("section")
    stabil_col = stabil[0].reshape(4, elem_count, 4, var_count, var_count)
    factor = factors[0, 0]

    def split_rows(row_block, number):
        parts = row_block.shape[0]
        inner_part = row_block[:, :, :inner_size]
        face_part = row_block[:, :, inner_size : inner_size + 4 * face_size].reshape(
            parts, number, 4, fnodes, var_count
        )
        trace_part = row_block[:, :, inner_size + 4 * face_size :].reshape(
            parts, number, 4, fnodes, var_count
        )
        return (inner_part, face_part, trace_part)

    def real_side(rows_in):
        row_block = rows_in.reshape(1, col_elems, row_width)
        inner_part, face_part, trace_part = split_rows(row_block, col_elems)
        inverse = factor.reshape(inner_size, col_elems, inner_size)

        def apply_real(right_sides):
            return jnp.einsum(
                "iej,crej->crei", inverse, right_sides, preferred_element_type=jnp.float32
            )

        result = condense(
            inner_part,
            face_part,
            trace_part,
            stabil_col.reshape(col_elems, 4, var_count, var_count),
            lift_matrix,
            face_matrix,
            apply_real,
        )
        result = result.reshape(1, 2, 4, elem_count, 4, fnodes, var_count)
        return jnp.concatenate([result, jnp.zeros((2,) + result.shape[1:], jnp.float32)], axis=0)

    def complex_side(rows_in):
        member = section_index - 1
        row_block = rows_in[:, : 2 * third_count * row_width].reshape(4, 2, third_count, row_width)
        row_block = row_block.transpose(1, 0, 2, 3).reshape(2, group_elems, row_width)
        inner_part, face_part, trace_part = split_rows(row_block, group_elems)
        picked = lax.dynamic_index_in_dim(
            stabil_col.reshape(4, third_count, 3, 4, var_count, var_count),
            member,
            axis=2,
            keepdims=False,
        )
        picked = picked.reshape(group_elems, 4, var_count, var_count)
        real_inverse = factor[:, : group_elems * inner_size].reshape(
            inner_size, group_elems, inner_size
        )
        imag_inverse = factor[:, group_elems * inner_size : 2 * group_elems * inner_size].reshape(
            inner_size, group_elems, inner_size
        )

        def apply_complex(right_sides):
            by_real = jnp.einsum(
                "iej,crej->crei", real_inverse, right_sides, preferred_element_type=jnp.float32
            )
            by_imag = jnp.einsum(
                "iej,crej->crei", imag_inverse, right_sides, preferred_element_type=jnp.float32
            )
            return jnp.stack([by_real[0] - by_imag[1], by_imag[0] + by_real[1]])

        result = condense(
            inner_part, face_part, trace_part, picked, lift_matrix, face_matrix, apply_complex
        )
        result = result.reshape(2, 2, 4, third_count, 1, 4, fnodes, var_count)
        select = (
            (jnp.arange(3, dtype=jnp.int32) == member)
            .astype(jnp.float32)
            .reshape(1, 1, 1, 1, 3, 1, 1, 1)
        )
        spread = (result * select).reshape(2, 2, 4, elem_count, 4, fnodes, var_count)
        return jnp.concatenate([jnp.zeros((1,) + spread.shape[1:], jnp.float32), spread], axis=0)

    contrib = lax.cond(section_index == 0, real_side, complex_side, received)
    node_order = orient[0].reshape(1, 1, 4, elem_count, 4, fnodes, 1)
    oriented = jnp.take_along_axis(contrib, node_order, axis=5)
    payload = oriented.transpose(2, 3, 4, 0, 1, 5, 6).reshape(16 * elem_count, payload_width)
    face_ids = element_faces[0].reshape(-1)
    owner_col = face_ids // face_dev % columns
    owned_slot = face_ids // (face_dev * columns) * face_dev + face_ids % face_dev
    column_index = lax.axis_index("elem")
    is_local = owner_col == column_index
    local_sum = jax.ops.segment_sum(
        payload, jnp.where(is_local, owned_slot, col_faces), col_faces + 1
    )[:col_faces]
    marks = (
        (owner_col[:, None] == jnp.arange(columns, dtype=jnp.int32)[None, :])
        & jnp.logical_not(is_local)[:, None]
    ).astype(jnp.int32)
    ranking = jnp.sum(marks * (jnp.cumsum(marks, axis=0) - 1), axis=1)
    slot_index = jnp.where(is_local, columns * share_slots, owner_col * share_slots + ranking)
    outgoing_items = jax.ops.segment_sum(payload, slot_index, columns * share_slots + 1)[:-1]
    outgoing_items = outgoing_items.reshape(columns, share_slots, payload_width)
    slot_faces = jax.ops.segment_sum(owned_slot + 1, slot_index, columns * share_slots + 1)[:-1] - 1
    slot_faces = slot_faces.reshape(columns, share_slots)
    got_items, got_faces = (
        lax.all_to_all(outgoing_items, "elem", split_axis=0, concat_axis=0, tiled=True),
        lax.all_to_all(slot_faces, "elem", split_axis=0, concat_axis=0, tiled=True),
    )
    targets = jnp.where(got_faces < 0, col_faces, got_faces).reshape(-1)
    remote_sum = jax.ops.segment_sum(
        got_items.reshape(columns * share_slots, payload_width), targets, col_faces + 1
    )[:col_faces]
    combined = local_sum + remote_sum
    owned_sums = lax.psum_scatter(combined, "section", scatter_dimension=0, tiled=True)
    owned_sums = owned_sums.reshape(face_dev, 3, 2, face_size)
    return (owned_sums[:, :, 0].transpose(1, 0, 2), owned_sums[:, :, 1].transpose(1, 0, 2))


def solution(mesh):
    return jax.shard_map(
        on_device,
        mesh=mesh,
        in_specs=(
            P(None, "elem", "section", None, None),
            P(None, "elem", "section", None, None, None),
            P(None, "elem", "section", None, None, None),
            P("elem", None, None, None, None),
            P("elem", None, None, None),
            P("elem", None, None, None, None),
            P(),
            P(),
            P("section", "elem", None, None),
        ),
        out_specs=(P(None, ("section", "elem"), None), P(None, ("section", "elem"), None)),
        check_vma=False,
    )
```

profile of v0, /device:TPU:0, one launch (start us, length us, event | category | flops | bytes accessed | tf_op | source)
XLA Modules:
  0.0 487.7 jit_solution(4384449431566786816)
XLA Ops:
  10.9 1.7 reduce-window.6
  13.8 5.8 %scatter_custom_fusion.1 = s32[17]{0:T(128)S(1)} fusion(s32[768]{0:T(1024)S(1)} %get-tuple-element.107, s32[768]{0:T(1024)S(1)} %fusion.88, s32[]{:T(128)} %constant.93.clone.1), kind=kCustom, calls=%fused_computation.140 | custom fusion | flops 768 | bytes 72 | tf_op jit(solution)/shard_map/scatter-add | solution.py:190
  20.3 6.3 %all-to-all-start.1 = ((s32[8,1,2]{2,1,0:T(1,128)}), s32[8,1,2]{2,1,0:T(1,128)S(1)}, u32[]{:S(2)}, u32[]{:S(2)}) async-start(s32[8,1,2]{2,1,0:T(1,128)} %bitcast.73), calls=%async_computation.1 | async-start | bytes 8192 | tf_op jit(solution)/shard_map/all_to_all | solution.py:194
  26.7 1.1 reshape.497
  27.8 1.1 reshape.496
  33.6 3.7 all-to-all-start
  39.5 3.3 all-to-all-done
  43.2 89.0 %conditional.1 = (f32[3,2,4,48,4,10,5]{6,1,5,4,3,2,0:T(2,128)}) conditional(s32[]{:T(128)} %convert_element_type.90, (bf16[4,24000]{1,0:T(4,128)(2,1)S(1)}, bf16[1,4,48,4,25]{2,3,4,1,0:T(4,128)(2,1)S(1)}, s32[]{:T(128)}, bf16[4,20,10]{1,0,2:T(4,128)(2,1)S(1)}, bf16[1,1,100,19200]{3,2,1,0:T(8,128)(2,1)}, ...), branch_computations={%region_0.1_spmd, %region_1.2_spmd} | conditional | flops 49900800 | bytes 25373970 | solution.py:170
  49.6 2.3 copy.321
  52.1 3.6 copy.322
  55.7 2.8 fusion.97
  58.6 21.1 %reshape_squeeze.8 = bf16[100,192,100]{2,1,0:T(8,128)(2,1)} reshape(bf16[1,1,100,19200]{3,2,1,0:T(8,128)(2,1)} %get-tuple-element.35) | data formatting | bytes 7680000 | tf_op jit(solution)/shard_map/cond/branch_1_fun/reshape;squeeze | solution.py:111
  79.6 2.1 fusion.61
  82.8 7.5 %fusion.52 = f32[1,2,192,100]{3,1,2,0:T(2,128)} fusion(bf16[100,192,100]{2,1,0:T(8,128)(2,1)} %reshape_squeeze.8, bf16[1,1,192,100]{3,1,2,0:T(2,128)(2,1)S(1)} %copy.326, bf16[1,1,192,100]{3,1,2,0:T(2,128)(2,1)S(1)} %copy.325), kind=kOutput, calls=%fused_computation.52 | convolution fusion | flops 7833600 | bytes 4070400 | tf_op jit(solution)/shard_map/cond/branch_1_fun/iej,crej->crei/dot_general | solution.py:114
  90.3 1.1 copy.328
  91.4 1.9 copy.376
  93.3 3.8 copy.377
  97.1 4.5 convolution_bitcast_fusion.2
  101.6 5.2 %fusion.43 = f32[1,2,192,4,10,5]{2,4,5,1,3,0:T(8,128)S(1)} fusion(f32[2,192,4,20,5]{3,4,2,0,1:T(8,128)S(1)} %convolution_bitcast_fusion.2, bf16[4,20,10]{1,0,2:T(4,128)(2,1)S(1)} %get-tuple-element.102), kind=kOutput, calls=%fused_computation.49 | convolution fusion | flops 18432000 | bytes 923200 | tf_op jit(solution)/shard_map/cond/branch_1_fun/kmn,crekmv->creknv/dot_general | solution.py:44
  106.8 2.7 fusion.49
  110.1 1.0 slice_subtract_fusion.2
  111.7 9.5 %copy.395 = f32[1,2,4,48,4,10,5]{6,1,5,4,3,2,0:T(2,128)} copy(f32[1,2,4,48,4,10,5]{3,2,4,6,5,1,0:T(4,128)S(1)} %pad_maximum_fusion.3) | data formatting | bytes 614400 | tf_op jit(solution)/shard_map/cond
  121.3 10.7 %concatenate.15.clone = f32[3,2,4,48,4,10,5]{6,1,5,4,3,2,0:T(2,128)} pad(f32[1,2,4,48,4,10,5]{6,1,5,4,3,2,0:T(2,128)} %copy.395, f32[]{:T(128)} %constant.60.clone), padding=0_2x0_0x0_0x0_0x0_0x0_0x0_0 | pad | bytes 1228804 | tf_op jit(solution)/shard_map/cond/branch_1_fun/concatenate | solution.py:128
  132.2 107.6 %gather_fusion = f32[7680,3,2,5]{3,2,1,0:T(2,128)} fusion(f32[3,2,4,48,4,10,5]{6,1,5,4,3,2,0:T(2,128)} %get-tuple-element.105, s32[7680]{0:T(1024)S(1)} %reshape.507), kind=kCustom, calls=%fused_computation | custom fusion | bytes 1966080 | tf_op jit(solution)/shard_map/jit(take_along_axis)/gather | solution.py:172
  239.8 43.0 %copy.390 = f32[4,48,4,10,3,2,5]{3,2,1,0,5,6,4:T(4,128)} copy(f32[4,48,4,10,3,2,5]{6,5,4,3,2,1,0:T(2,128)} %bitcast.222) | data formatting | bytes 1843200 | tf_op jit(solution)/shard_map/jit(take_along_axis)/gather | solution.py:172
  282.8 12.3 %select_bitcast_fusion = f32[4,48,4,3,2,10,5]{5,2,1,0,4,6,3:T(4,128)} fusion(f32[4,48,4,10,3,2,5]{3,2,1,0,5,6,4:T(4,128)} %copy.390, pred[4,48,4,10]{3,2,1,0:T(4,128)(4,1)S(1)} %copy-done.8), kind=kLoop, calls=%fused_computation.68 | loop fusion | flops 230400 | bytes 1850880 | tf_op jit(solution)/shard_map/jit(take_along_axis)/select_n | solution.py:172
  295.1 41.2 %copy.352 = f32[4,48,4,3,2,10,5]{2,1,0,6,5,4,3:T(8,128)} copy(f32[4,48,4,3,2,10,5]{5,2,1,0,4,6,3:T(4,128)} %select_bitcast_fusion) | data formatting | bytes 1843200 | tf_op jit(solution)/shard_map/jit(take_along_axis)/select_n | solution.py:172
  336.3 25.8 %reshape.533 = f32[768,300]{0,1:T(8,128)S(1)} reshape(f32[4,48,4,3,2,10,5]{2,1,0,6,5,4,3:T(8,128)} %copy.352) | data formatting | bytes 1843200 | tf_op jit(solution)/shard_map/reshape | solution.py:173
  362.5 7.4 %scatter_custom_fusion.2 = f32[17,300]{1,0:T(8,128)S(1)} fusion(s32[768]{0:T(1024)} %copy-done.12, f32[768,300]{1,0:T(8,128)S(1)} %copy.353, f32[]{:T(128)} %constant.90.clone.1), kind=kCustom, calls=%fused_computation.99 | custom fusion | flops 230400 | bytes 20912 | tf_op jit(solution)/shard_map/scatter-add | solution.py:188
  370.6 4.8 all-to-all-start.2
  375.7 6.8 %scatter_custom_fusion = f32[385,300]{1,0:T(8,128)S(1)} fusion(s32[768]{0:T(1024)} %get-tuple-element.106, f32[768,300]{1,0:T(8,128)S(1)} %copy.353, f32[]{:T(128)} %constant.90.clone.1), kind=kCustom, calls=%fused_computation.74 | custom fusion | flops 230400 | bytes 462512 | tf_op jit(solution)/shard_map/scatter-add | solution.py:179
  384.4 94.3 %reduce-scatter.2.cloned.1.call-done = f32[96,300]{1,0:T(8,128)} async-done(((f32[384,300]{1,0:T(8,128)}), f32[96,300]{1,0:T(8,128)}) %reduce-scatter.2.cloned.1.call-update) | async-done | bytes 115216 | tf_op jit(solution)/shard_map/reduce_scatter | solution.py:201
  (102 shorter events, 21.2 us)
Async XLA Ops:
  7.2 25.7 %copy-start.9 = (s32[1,4,48,4,10]{2,3,4,1,0:T(4,128)S(1)}, s32[1,4,48,4,10]{2,3,4,1,0:T(4,128)}, u32[]{:S(2)}) copy-start(s32[1,4,48,4,10]{2,3,4,1,0:T(4,128)} %param.16) | copy-start | bytes 92164
  13.8 16.2 %copy-start.12 = (s32[768]{0:T(1024)}, s32[768]{0:T(1024)S(1)}, u32[]{:S(2)}) copy-start(s32[768]{0:T(1024)S(1)} %get-tuple-element.107) | copy-start | bytes 9220
  20.3 13.3 %all-to-all-start.1 = ((s32[8,1,2]{2,1,0:T(1,128)}), s32[8,1,2]{2,1,0:T(1,128)S(1)}, u32[]{:S(2)}, u32[]{:S(2)}) async-start(s32[8,1,2]{2,1,0:T(1,128)} %bitcast.73), calls=%async_computation.1 | async-start | bytes 8192 | tf_op jit(solution)/shard_map/all_to_all | solution.py:194
  26.6 16.5 %copy-start.6 = (bf16[4,20,10]{1,0,2:T(4,128)(2,1)S(1)}, bf16[4,20,10]{1,0,2:T(4,128)(2,1)}, u32[]{:S(2)}) copy-start(bf16[4,20,10]{1,0,2:T(4,128)(2,1)} %param.17) | copy-start | bytes 4804
  26.7 16.5 %copy-start.7 = (bf16[1,4,48,4,25]{2,3,4,1,0:T(4,128)(2,1)S(1)}, bf16[1,4,48,4,25]{2,3,4,1,0:T(4,128)(2,1)}, u32[]{:S(2)}) copy-start(bf16[1,4,48,4,25]{2,3,4,1,0:T(4,128)(2,1)} %param.14) | copy-start | bytes 115204
  26.7 16.5 %copy-start.11 = (bf16[10,10]{1,0:T(8,128)(2,1)S(1)}, bf16[10,10]{1,0:T(8,128)(2,1)}, u32[]{:S(2)}) copy-start(bf16[10,10]{1,0:T(8,128)(2,1)} %param.18) | copy-start | bytes 604
  33.6 9.2 %all-to-all-start = ((bf16[4,2,12000]{2,1,0:T(2,128)(2,1)}), bf16[4,2,12000]{2,1,0:T(2,128)(2,1)S(1)}, u32[]{:S(2)}, u32[]{:S(2)}) async-start(bf16[4,2,12000]{2,1,0:T(2,128)(2,1)} %reshape.579), calls=%async_computation | async-start | bytes 385024 | tf_op jit(solution)/shard_map/all_to_all | solution.py:92
  48.7 3.5 copy-start.2
  101.6 8.3 %copy-start.3 = (f32[1,192,200]{2,1,0:T(8,128)S(1)}, f32[1,192,200]{2,1,0:T(8,128)}, u32[]{:S(2)}) copy-start(f32[1,192,200]{2,1,0:T(8,128)} %get-tuple-element.120) | copy-start | bytes 460804 | tf_op jit(solution)/shard_map/cond
  106.8 2.7 copy-start.1
  239.8 43.0 %copy-start.8 = (pred[4,48,4,10]{3,2,1,0:T(4,128)(4,1)S(1)}, pred[4,48,4,10]{3,2,1,0:T(4,128)(4,1)}, u32[]{:S(2)}) copy-start(pred[4,48,4,10]{3,2,1,0:T(4,128)(4,1)} %copy.342) | copy-start | bytes 23044
  370.6 12.0 %all-to-all-start.2 = ((f32[8,2,300]{2,1,0:T(2,128)}), f32[8,2,300]{2,1,0:T(2,128)S(1)}, u32[]{:S(2)}, u32[]{:S(2)}) async-start(f32[8,2,300]{2,1,0:T(2,128)} %reshape.502), calls=%async_computation.2 | async-start | bytes 49152 | tf_op jit(solution)/shard_map/all_to_all | solution.py:193
  375.4 103.3 %reduce-scatter.2.cloned.1.call-start = ((), (), s32[]{:S(2)}) async-start(), calls=%async_computation.4 | async-start | bytes 737280 | tf_op jit(solution)/shard_map/reduce_scatter | solution.py:201
Sparse Core Ops, SparseCore 0:
  384.5 94.1 reduce-scatter.1
where the time goes:
time: 494 us; the launch traced here: 488 us
  local copies, waits for them, and re-layouts  287 us (58%)
  waiting for transfers between devices  97.6 us (20%)
  other arithmetic  43.1 us (9%)
  matrix products  24.8 us (5%)
  starting transfers between devices  15.2 us (3%)
  between operations  14.9 us (3%)
  loops' own time  5.5 us (1%)
    gather x4, local copies, waits for them, and re-layouts, on_device(): oriented = jnp.take_along_axis(contrib, node_order, axis=5)  151 us
    reduce_scatter x1, waiting for transfers between devices, on_device(): lax.psum_scatter(combined, 'section', scatter_dimension=0, tiled=True)  94.3 us
    select_n x1, local copies, waits for them, and re-layouts, on_device(): oriented = jnp.take_along_axis(contrib, node_order, axis=5)  41.2 us
    reshape x2, local copies, waits for them, and re-layouts, on_device(): oriented.transpose(2, 3, 4, 0, 1, 5, 6)  26.2 us
    another operation x1, local copies, waits for them, and re-layouts, real_side(): inverse = factor.reshape(inner_size, col_elems, inner_size)  21.1 us
    select_n x1, other arithmetic, on_device(): oriented = jnp.take_along_axis(contrib, node_order, axis=5)  12.3 us
    concatenate x1, local copies, waits for them, and re-layouts, real_side(): jnp.concatenate([result, jnp.zeros((2,) + result.shape[1:], jnp.float32)]...  10.7 us
  transfers between devices with their start and end apart: 4, of which 2 were waited for; matrix products, arithmetic and copies ran while one was open for 3% of the time, Pallas kernels for 0%

commit v1 on v0

v1 whole, which is shorter than its diff:
```python
import functools

import jax
import jax.numpy as jnp
import numpy as np
from jax import lax
from jax.experimental import pallas as pl
from jax.experimental.pallas import tpu as pltpu
from jax.sharding import PartitionSpec as P

radau_inverse = (
    (4.325579890063155, 0.33919925181580984, 0.5417705399358749),
    (-4.178718591551905, -0.32768282076106237, 0.47662355450055044),
    (-0.5028726349457868, 2.571926949855605, -0.5960392048282249),
)
LANE = 128
HALF = 64
MESH = pl.DeviceIdType.MESH


def triangle_table(fnodes):
    degree = next(d for d in range(1, fnodes) if (d + 1) * (d + 2) // 2 == fnodes)
    lattice = [(a, b, degree - a - b) for a in range(degree + 1) for b in range(degree + 1 - a)]
    rotations = [(0, 1, 2), (1, 2, 0), (2, 0, 1), (0, 2, 1), (2, 1, 0), (1, 0, 2)]
    return [
        [lattice.index(tuple(point[corner] for corner in rotation)) for point in lattice]
        for rotation in rotations
    ]


def structure(modes, fnodes, nvar, elems, chunk):
    lane = np.arange(LANE)
    side, inside = lane // HALF, lane % HALF
    node, var = inside // nvar, inside % nvar
    used = inside < fnodes * nvar
    inner = modes * nvar
    parts, place, at = [], {}, 0

    def add(name, block):
        nonlocal at
        rows, cols = block.shape
        wide = -(-cols // LANE) * LANE
        full = np.zeros((LANE, wide), np.float32)
        full[:rows, :cols] = block
        place[name] = (at, at + wide)
        parts.append(full)
        at += wide

    row = lane[:, None]
    expand, shifts, top, bottom = [], [], [], []
    for d in range(nvar):
        other = (var + d) % nvar
        expand.append((row == (var * nvar + other)[None]) & used[None])
        shifts.append(
            (row == (side * HALF + node * nvar + other)[None]) & (used & (side == 1))[None]
        )
        fit = (row % nvar == other[None]) & used[None] & (row < inner)
        top.append(fit & (side == 0)[None])
        bottom.append(fit & (side == 1)[None])
    expand.append((row == nvar * nvar) & np.ones((1, LANE), bool))
    add("expand", np.concatenate(expand, 1))
    add("shifts", np.concatenate(shifts, 1))
    add("top", np.concatenate(top, 1))
    add("bottom", np.concatenate(bottom, 1))
    add("modes", (row // nvar == np.arange(modes)[None]) & (row < inner))
    nodes = (np.arange(fnodes)[:, None] == node[None]) & used[None]
    add("nodes", np.concatenate([nodes] * nvar, 1))
    add("rows_node", nodes.T)
    one = used & (side == 1)
    add("same", (var[:, None] == var[None]) & one[:, None] & one[None])
    table = triangle_table(fnodes)
    turns = []
    for order in table:
        order = np.array(order + [0] * HALF)
        source = side * HALF + order[node] * nvar + var
        turns.append((row == source[None]) & used[None])
    add("turns", np.concatenate(turns, 1))
    column = np.arange(chunk * inner)
    add("repeat", row == (column % inner)[None])
    third = elems // 3
    r = np.arange(elems)
    add("thirds", (3 * (r % third) + r // third)[:, None] == r[None])
    return np.concatenate(parts, 1), place, [order[1] for order in table]


def dot(a, b):
    return jnp.dot(a, b, preferred_element_type=jnp.float32)


def dot_nt(a, b):
    return lax.dot_general(a, b, (((1,), (1,)), ((), ())), preferred_element_type=jnp.float32)


def split(x):
    high = x.astype(jnp.bfloat16)
    low = (x - high.astype(jnp.float32)).astype(jnp.bfloat16)
    return jnp.concatenate([high, low], axis=0)


def kernel(
    dims,
    place,
    classes,
    pack_ref,
    meta_ref,
    ids_ref,
    lift_ref,
    face_ref,
    const_ref,
    factor_hbm,
    out_res,
    out_schur,
    factor,
    send1,
    recv1,
    weights,
    stab,
    base,
    solved,
    send2,
    recv2,
    sums,
    send3,
    recv3,
    factor_sem,
    s1,
    r1,
    s2,
    r2,
    s3,
    r3,
):
    sections, columns, elems, inner, face_size, nvar, chunk = dims
    third = elems // 3
    col_elems = sections * elems
    face_dev = 2 * elems
    col_faces = sections * face_dev
    width = nvar * LANE
    f32, bf16 = jnp.float32, jnp.bfloat16
    section = lax.axis_index("section")
    column = lax.axis_index("elem")

    def const(name):
        lo, hi = place[name]
        return const_ref[:, lo:hi]

    factor_copy = pltpu.make_async_copy(factor_hbm.at[0, 0], factor, factor_sem)
    factor_copy.start()
    barrier = pltpu.get_barrier_semaphore()
    for d in range(1, sections):
        pl.semaphore_signal(
            barrier, inc=1, device_id={"section": lax.rem(section + d, sections)}, device_id_type=MESH
        )

    def greet(d, carry):
        pl.semaphore_signal(
            barrier, inc=1, device_id={"elem": lax.rem(column + d, columns)}, device_id_type=MESH
        )
        return carry

    lax.fori_loop(1, columns, greet, 0)

    send1[...] = jnp.zeros(send1.shape, bf16)
    thirds = const("thirds")[:elems, :elems]
    for part in range(5):
        values = [pack_ref[t, part].astype(f32) for t in range(3)]
        for g in range(3):
            row = radau_inverse[g]
            w = (row[0] * values[0] + row[1] * values[1] + row[2] * values[2]).astype(bf16)
            if g == 0:
                send1[0, part] = w
            else:
                w = dot(thirds, w).astype(bf16)
                for t in range(3):
                    send1[1 + t, part, (g - 1) * third : g * third] = w[t * third : (t + 1) * third]

    pl.semaphore_wait(barrier, sections - 1 + columns - 1)

    def exchange(source, target, send_sem, recv_sem):
        copies = []
        for d in range(1, sections):
            peer = lax.rem(section + d, sections)
            copy = pltpu.make_async_remote_copy(
                src_ref=source.at[peer],
                dst_ref=target.at[section],
                send_sem=send_sem.at[d],
                recv_sem=recv_sem.at[d],
                device_id={"section": peer},
                device_id_type=MESH,
            )
            copy.start()
            copies.append(copy)
        return copies

    copies1 = exchange(send1, recv1, s1, r1)
    recv1[section] = send1[section]

    for k in range(4):
        by_node = dot(lift_ref[k], const("nodes")[: lift_ref.shape[2]]).astype(bf16)
        wide = dot(const("modes")[:, : lift_ref.shape[1]], by_node).astype(bf16)
        weights[k, :LANE] = wide * const("top")
        weights[k, LANE:] = wide * const("bottom")
    rows_node = const("rows_node")[:, : face_ref.shape[0]]
    face_rows = dot(rows_node, face_ref[...]).astype(bf16)
    face_wide = (dot_nt(face_rows, rows_node) * const("same").astype(f32)).astype(bf16)
    solved[...] = jnp.zeros(solved.shape, f32)
    send3[...] = jnp.zeros(send3.shape, f32)

    for copy in copies1:
        copy.wait()
    factor_copy.wait()

    lane = lax.broadcasted_iota(jnp.int32, (1, LANE), 1)

    def apply_blocks(right, start):
        count = right.shape[0]
        wide = dot(right, const("repeat")).astype(bf16)
        place_row = lax.broadcasted_iota(jnp.int32, (count, chunk * inner), 0) % chunk * inner
        at = lax.broadcasted_iota(jnp.int32, (count, chunk * inner), 1) - place_row
        wide = jnp.where((at >= 0) & (at < inner), wide.astype(f32), 0.0).astype(bf16)
        blocks = []
        for begin in start:
            blocks.append(dot_nt(wide, factor[:, begin : begin + chunk * inner]))
        return blocks

    def work(parts, number, take, metas, ids):
        total = parts * number
        lifted = [None] * parts
        for k in range(4):
            stab[k, :number] = dot(metas[k], const("expand"))
            for c in range(parts):
                traced = take(c, 1 + k)
                shifted = dot(traced, const("shifts"))
                weighted = jnp.zeros((number, LANE), f32)
                for d in range(nvar):
                    weighted += (
                        stab[k, :number, d * LANE : (d + 1) * LANE]
                        * shifted[:, d * LANE : (d + 1) * LANE]
                    )
                pair = split(weighted)
                term = dot_nt(pair, weights[k, LANE:, :LANE])
                term = term[:number] + term[number:]
                lifted[c] = term if k == 0 else lifted[c] + term
                own = dot_nt(pair, face_wide)
                own = own[:number] + own[number:]
                base[k, c * number : (c + 1) * number] = jnp.where(
                    lane < HALF, traced.astype(f32), own
                )
        lifted = [x.astype(bf16) for x in lifted]
        inners = [take(c, 0) for c in range(parts)]
        for begin in range(0, number, chunk):
            cut = slice(begin, begin + chunk)
            rights = [x[cut] for x in inners] + [x[cut] for x in lifted]
            right = jnp.concatenate(rights, axis=0)
            if parts == 1:
                (got,) = apply_blocks(right, [begin * inner])
                for side in range(2):
                    solved[cut, side * LANE : side * LANE + inner] = got[
                        side * chunk : (side + 1) * chunk
                    ]
            else:
                by_real, by_imag = apply_blocks(right, [begin * inner, (number + begin) * inner])
                for side in range(2):
                    a = slice(2 * side * chunk, (2 * side + 1) * chunk)
                    b = slice((2 * side + 1) * chunk, (2 * side + 2) * chunk)
                    lanes = slice(side * LANE, side * LANE + inner)
                    solved[cut, lanes] = by_real[a] - by_imag[b]
                    solved[number + begin : number + begin + chunk, lanes] = by_imag[a] + by_real[b]
        pair = split(solved[:total])
        owner, slot = ids
        rows = columns * 8
        row = lax.broadcasted_iota(jnp.int32, (rows, 1), 0)
        row_col = (row // 8).astype(f32)
        item = row % 8
        index = lax.broadcasted_iota(jnp.int32, (1, number), 1).astype(f32)
        mine = column.astype(f32)
        far = float(8 * col_elems)
        least = jnp.full((rows, 1), far, f32)
        most = jnp.full((rows, 1), -1.0, f32)
        for k in range(4):
            mark = (owner[k : k + 1] == row_col) & (row_col != mine)
            least = jnp.minimum(
                least, jnp.min(jnp.where(mark, index + k * number, far), 1, keepdims=True)
            )
            most = jnp.maximum(
                most, jnp.max(jnp.where(mark, index + k * number, -1.0), 1, keepdims=True)
            )
        wanted = jnp.where(item % 2 == 0, least, jnp.where(most > least, most, -1.0))
        faces = lax.broadcasted_iota(jnp.int32, (col_faces, 1), 0).astype(f32)
        numbers = jnp.zeros((rows, 1), f32)
        items = jnp.zeros((rows, LANE), f32)
        local = [jnp.zeros((col_faces, LANE), f32) for _ in range(parts)]
        for k in range(4):
            mixed = dot(pair, weights[k])
            mixed = mixed[:total] + mixed[total:]
            local_slot = jnp.where(owner[k : k + 1] == mine, slot[k : k + 1], -1.0)
            spread = jnp.where(faces == local_slot, 1.0, 0.0).astype(bf16)
            chosen = jnp.where(index + k * number == wanted, 1.0, 0.0)
            numbers += jnp.sum(chosen * (slot[k : k + 1] + 1.0), 1, keepdims=True)
            for c in range(parts):
                cut = slice(c * number, (c + 1) * number)
                pay = base[k, cut]
                for d in range(nvar):
                    pay -= (
                        stab[k, :number, d * LANE : (d + 1) * LANE]
                        * mixed[cut, d * LANE : (d + 1) * LANE]
                    )
                turned = dot(pay.astype(bf16), const("turns"))
                kind = stab[k, :number, width : width + LANE]
                result = jnp.zeros((number, LANE), f32)
                for place_in, name in enumerate(classes):
                    result = jnp.where(
                        kind == float(name), turned[:, place_in * LANE : (place_in + 1) * LANE], result
                    )
                result = result.astype(bf16)
                local[c] += dot(spread, result)
                picked = jnp.where(item // 2 == c, chosen, 0.0).astype(bf16)
                items += dot(picked, result)
        numbers = jnp.where(item < 2 * parts, numbers - 1.0, -1.0)
        items = jnp.where(lane == HALF - 1, numbers, items)
        send2[...] = items.reshape(columns, 8, LANE)
        for c in range(parts):
            sums[c] = local[c]
        if parts == 1:
            sums[1] = jnp.zeros((col_faces, LANE), f32)

    @pl.when(section == 0)
    def _():
        def take(c, part):
            return jnp.concatenate([recv1[s, part] for s in range(sections)], axis=0)

        ids = ids_ref[...].astype(f32)
        work(1, col_elems, take, [meta_ref[k] for k in range(4)], (ids[:4], ids[4:8] * 16 + ids[8:12]))

    @pl.when(section != 0)
    def _():
        number = sections * third
        r = lax.broadcasted_iota(jnp.int32, (number, col_elems), 0)
        e = lax.broadcasted_iota(jnp.int32, (number, col_elems), 1)
        wanted = r // third * elems + r % third * 3 + (section - 1)
        pick = jnp.where(e == wanted, 1.0, 0.0).astype(bf16)

        def take(c, part):
            return jnp.concatenate(
                [recv1[s, part, c * third : (c + 1) * third] for s in range(sections)], axis=0
            )

        ids = dot_nt(ids_ref[...], pick)
        metas = [dot(pick, meta_ref[k]).astype(bf16) for k in range(4)]
        work(2, number, take, metas, (ids[:4], ids[4:8] * 16 + ids[8:12]))

    def item_copy(d):
        peer = lax.rem(column + d, columns)
        return pltpu.make_async_remote_copy(
            src_ref=send2.at[peer],
            dst_ref=recv2.at[column],
            send_sem=s2.at[d],
            recv_sem=r2.at[d],
            device_id={"elem": peer},
            device_id_type=MESH,
        )

    def start_item(d, carry):
        item_copy(d).start()
        return carry

    def end_item(d, carry):
        item_copy(d).wait()
        return carry

    lax.fori_loop(1, columns, start_item, 0)
    recv2[column] = send2[column]
    lax.fori_loop(1, columns, end_item, 0)
    arrived = recv2[...].reshape(columns * 8, LANE)
    item = lax.broadcasted_iota(jnp.int32, (columns * 8, 1), 0) % 8
    numbers = arrived[:, HALF - 1 : HALF]
    faces = lax.broadcasted_iota(jnp.int32, (1, col_faces), 1).astype(f32)
    for c in range(2):
        hits = jnp.where((numbers == faces) & (item // 2 == c), 1.0, 0.0)
        spread = jnp.transpose(hits).astype(bf16)
        full = sums[c] + dot(spread, arrived.astype(bf16))
        for s in range(sections):
            send3[s, c] = full[s * face_dev : (s + 1) * face_dev]

    copies3 = exchange(send3, recv3, s3, r3)
    recv3[section] = send3[section]
    for copy in copies3:
        copy.wait()
    first = recv3[0, 0]
    second, third_part = recv3[1, 0], recv3[1, 1]
    for s in range(2, sections):
        second += recv3[s, 0]
        third_part += recv3[s, 1]
    for g, total in enumerate((first, second, third_part)):
        out_res[g] = total[:, :face_size]
        out_schur[g] = total[:, HALF : HALF + face_size]


def on_device(
    interior_res,
    face_res,
    trace_vals,
    stabil,
    element_faces,
    orient,
    lift_matrix,
    face_matrix,
    factors,
):
    sections = lax.axis_size("section")
    columns = lax.axis_size("elem")
    elems, inner = interior_res.shape[3:]
    face_size = face_res.shape[5]
    fnodes = face_matrix.shape[0]
    modes = lift_matrix.shape[1]
    nvar = face_size // fnodes
    chunk = 32
    col_elems = sections * elems
    face_dev = 2 * elems
    col_faces = sections * face_dev
    f32, bf16 = jnp.float32, jnp.bfloat16
    consts, place, classes = structure(modes, fnodes, nvar, elems, chunk)

    def widen(x, size):
        return jnp.pad(x, [(0, 0)] * (x.ndim - 1) + [(0, size - x.shape[-1])])

    sides = jnp.concatenate(
        [widen(face_res[:, 0, 0], HALF), widen(trace_vals[:, 0, 0], HALF)], axis=-1
    ).transpose(0, 2, 1, 3)
    pack = jnp.concatenate([widen(interior_res[:, 0], LANE), sides], axis=1)
    meta = jnp.concatenate([stabil[0], orient[0, :, :, :, 1:2].astype(bf16)], axis=-1)
    meta = widen(meta.reshape(col_elems, 4, nvar * nvar + 1).transpose(1, 0, 2), LANE)
    face = element_faces[0].reshape(col_elems, 4).transpose(1, 0)
    slot = face // (face_dev * columns) * face_dev + face % face_dev
    ids = jnp.concatenate(
        [face // face_dev % columns, slot // 16, slot % 16, jnp.zeros_like(slot)], axis=0
    ).astype(bf16)
    dims = (sections, columns, elems, inner, face_size, nvar, chunk)
    out = jax.ShapeDtypeStruct((3, face_dev, face_size), f32)
    vmem = pl.BlockSpec(memory_space=pltpu.VMEM)
    return pl.pallas_call(
        functools.partial(kernel, dims, place, classes),
        out_shape=(out, out),
        in_specs=[vmem] * 6 + [pl.BlockSpec(memory_space=pl.ANY)],
        out_specs=(vmem, vmem),
        scratch_shapes=[
            pltpu.VMEM(factors.shape[2:], bf16),
            pltpu.VMEM((sections, 5, elems, LANE), bf16),
            pltpu.VMEM((sections, 5, elems, LANE), bf16),
            pltpu.VMEM((4, 2 * LANE, nvar * LANE), bf16),
            pltpu.VMEM((4, col_elems, (nvar + 1) * LANE), f32),
            pltpu.VMEM((4, col_elems, LANE), f32),
            pltpu.VMEM((col_elems, 2 * LANE), f32),
            pltpu.VMEM((columns, 8, LANE), f32),
            pltpu.VMEM((columns, 8, LANE), f32),
            pltpu.VMEM((2, col_faces, LANE), f32),
            pltpu.VMEM((sections, 2, face_dev, LANE), f32),
            pltpu.VMEM((sections, 2, face_dev, LANE), f32),
            pltpu.SemaphoreType.DMA,
            pltpu.SemaphoreType.DMA((sections,)),
            pltpu.SemaphoreType.DMA((sections,)),
            pltpu.SemaphoreType.DMA((columns,)),
            pltpu.SemaphoreType.DMA((columns,)),
            pltpu.SemaphoreType.DMA((sections,)),
            pltpu.SemaphoreType.DMA((sections,)),
        ],
        compiler_params=pltpu.CompilerParams(
            collective_id=0, has_side_effects=True, vmem_limit_bytes=56 * 2**20
        ),
    )(pack, meta, ids, lift_matrix, face_matrix, jnp.asarray(consts, bf16), factors)


def solution(mesh):
    return jax.shard_map(
        on_device,
        mesh=mesh,
        in_specs=(
            P(None, "elem", "section", None, None),
            P(None, "elem", "section", None, None, None),
            P(None, "elem", "section", None, None, None),
            P("elem", None, None, None, None),
            P("elem", None, None, None),
            P("elem", None, None, None, None),
            P(),
            P(),
            P("section", "elem", None, None),
        ),
        out_specs=(P(None, ("section", "elem"), None), P(None, ("section", "elem"), None)),
        check_vma=False,
    )
```

time: 494 us -> 42.4 us (0.09); the launches traced: 488 us -> 41.9 us
  local copies, waits for them, and re-layouts: 287 us -> 8.36 us
  waiting for transfers between devices: 97.6 us -> 0 us
  other arithmetic: 43.1 us -> 4.46 us
  Pallas kernels: 0 us -> 28.4 us
  matrix products: 24.8 us -> 0 us
  starting transfers between devices: 15.2 us -> 0 us
  between operations: 14.9 us -> 0.71 us
  loops' own time: 5.5 us -> 0 us
    gather x4 -> x0, local copies, waits for them, and re-layouts: 151 us -> none  [on_device(): oriented = jnp.take_along_axis(contrib, node_order, axis=5)]
    reduce_scatter x1 -> x0, waiting for transfers between devices: 94.3 us -> none  [on_device(): lax.psum_scatter(combined, 'section', scatter_dimension=0, tiled=True)]
    select_n x1 -> x0, local copies, waits for them, and re-layouts: 41.2 us -> none  [on_device(): oriented = jnp.take_along_axis(contrib, node_order, axis=5)]
    another operation x15 -> x0, local copies, waits for them, and re-layouts: 34.6 us -> none  [the longest x1 21.1 us: real_side(): inverse = factor.reshape(inner_size, col_elems, inner_size)]
    reshape x9 -> x0, local copies, waits for them, and re-layouts: 29.7 us -> none  [the longest x2 26.2 us: on_device(): oriented.transpose(2, 3, 4, 0, 1, 5, 6)]
    pallas_call x0 -> x1, Pallas kernels: none -> 28.4 us  [on_device(): pl.pallas_call(functools.partial(kernel, dims, place, classes), out_shape...]
    dot_general x6 -> x0, matrix products: 24.8 us -> none  [the longest x1 7.5 us: apply_real(): jnp.einsum('iej,crej->crei', inverse, right_sides, preferred_element_type...]
    scatter-add x4 -> x0, other arithmetic: 20.9 us -> none  [the longest x1 7.4 us: on_device(): jax.ops.segment_sum(payload, slot_index, columns * share_slots + 1)[:-1]]
  transfers between devices with their start and end apart: 4 -> 0, of which waited for: 2 -> 0; matrix products, arithmetic and copies ran while one was open for 3% -> 0% of each run, Pallas kernels for 0% -> 0%
where the time goes in v1:
time: 42.4 us; the launch traced here: 41.9 us
  Pallas kernels  28.4 us (67%)
  local copies, waits for them, and re-layouts  8.36 us (20%)
  other arithmetic  4.46 us (11%)
  between operations  0.71 us (2%)
    pallas_call x1, Pallas kernels, on_device(): pl.pallas_call(functools.partial(kernel, dims, place, classes), out_shape...  28.4 us
    pallas_call x2, local copies, waits for them, and re-layouts, on_device(): pl.pallas_call(functools.partial(kernel, dims, place, classes), out_shape...  3.32 us
    unnamed x2, local copies, waits for them, and re-layouts  2.36 us
    concatenate x1, other arithmetic, on_device(): pack = jnp.concatenate([widen(interior_res[:, 0], LANE), sides], axis=1)  1.46 us
    squeeze x1, local copies, waits for them, and re-layouts, on_device(): trace_vals[:, 0, 0]  1.02 us

profile of v1, /device:TPU:0, one launch (start us, length us, event | category | flops | bytes accessed | tf_op | source)
XLA Modules:
  0.0 41.9 jit_solution(13066081148765654751)
XLA Ops:
  0.6 0.1 pad.22.clone
  0.7 0.7 %slice_convert_fusion = bf16[1,4,48,4,1]{2,3,4,1,0:T(4,128)(2,1)S(1)} fusion(s32[1,4,48,4,10]{2,3,4,1,0:T(4,128)} %param.15), kind=kLoop, calls=%fused_computation.12 | loop fusion | flops 768 | bytes 4608 | tf_op jit(solution)/shard_map/convert.4
  1.4 0.1 convert_element_type.21
  1.5 0.7 %sign_compare_fusion = (pred[1,4,48,4]{2,3,1,0:T(4,128)(4,1)S(1)}, pred[1,4,48,4]{2,3,1,0:T(4,128)(4,1)S(1)}) fusion(s32[1,4,48,4]{2,3,1,0:T(4,128)} %param.14), kind=kLoop, calls=%fused_computation.15 | loop fusion | flops 3072 | bytes 4608 | tf_op jit(solution)/shard_map/jit(floor_divide)/ne | solution.py:436
  2.2 0.1 ne.64
  2.3 0.1 ne.71
  2.4 1.4 %copy.47.lift_ref = bf16[4,20,10]{2,1,0:T(8,128)(2,1)} copy(bf16[4,20,10]{1,0,2:T(4,128)(2,1)} %param.16) | data formatting | bytes 3200 | tf_op args[6]
  3.9 0.7 %broadcast_divide_fusion.1 = (s32[1,4,48,4]{2,3,1,0:T(4,128)S(1)}, s32[1,4,48,4]{2,3,1,0:T(4,128)S(1)}, s32[1,4,48,4]{2,3,1,0:T(4,128)S(1)}) fusion(s32[1,4,48,4]{2,3,1,0:T(4,128)} %param.14), kind=kLoop, calls=%fused_computation.37 | loop fusion | flops 2304 | bytes 12288 | tf_op jit(solution)/shard_map/jit(floor_divide)/div | solution.py:436
  4.6 0.1 div.33
  4.7 0.1 rem.68
  4.8 0.1 div.36
  4.9 0.7 %maximum_maximum_fusion.ids_ref = bf16[16,192]{1,0:T(8,128)(2,1)} fusion(bf16[4,192]{1,0:T(4,128)(2,1)S(1)} %fusion.11, bf16[4,192]{1,0:T(4,128)(2,1)S(1)} %get-tuple-element.8, bf16[4,192]{1,0:T(4,128)(2,1)S(1)} %get-tuple-element.15, bf16[16]{0:T(256)(128)(2,1)S(1)} %pad.22.clone), kind=kLoop, calls=%fused_computation.13 | loop fusion | flops 24576 | bytes 10784 | tf_op jit(solution)/shard_map/concatenate | solution.py:435
  5.6 0.9 %copy.39 = bf16[1,4,48,4,25]{2,1,3,4,0:T(4,128)(2,1)S(1)} copy(bf16[1,4,48,4,25]{2,3,4,1,0:T(4,128)(2,1)} %param.13) | data formatting | bytes 76800 | tf_op args[3]
  6.5 0.1 concatenate.18
  6.7 0.2 copy.41
  6.9 0.7 %pad.18.meta_ref = bf16[4,192,128]{2,1,0:T(8,128)(2,1)} pad(bf16[4,192,26]{2,1,0:T(8,128)(2,1)S(1)} %bitcast.55, bf16[]{:T(256)} %constant.54.clone.1), padding=0_0x0_0x0_102 | pad | bytes 236546 | tf_op jit(solution)/shard_map/jit(_pad)/pad | solution.py:425
  7.6 1.0 %copy_bitcast_fusion = (bf16[3,48,4,50]{3,1,2,0:T(8,128)(2,1)S(1)}, bf16[3,48,4,50]{3,1,2,0:T(8,128)(2,1)S(1)}) fusion(bf16[3,1,1,48,4,50]{5,4,3,2,1,0:T(4,128)(2,1)} %param.12, bf16[3,1,1,48,4,50]{5,4,3,2,1,0:T(4,128)(2,1)} %param.11), kind=kLoop, calls=%fused_computation.9 | loop fusion | bytes 230400 | tf_op jit(solution)/shard_map/squeeze | solution.py:428
  8.6 0.1 fusion.5
  8.7 1.5 %fusion.3.pack_ref = bf16[3,5,48,128]{3,2,1,0:T(8,128)(2,1)} fusion(bf16[3,1,48,100]{3,2,1,0:T(8,128)(2,1)} %bitcast.56, bf16[3,4,48,128]{3,2,1,0:T(8,128)(2,1)S(1)} %fusion.5), kind=kLoop, calls=%fused_computation.6 | loop fusion | flops 552960 | bytes 360576 | tf_op jit(solution)/shard_map/concatenate | solution.py:430
  10.2 28.4 %shard_map.113 = (f32[3,96,50]{2,1,0:T(8,128)}, f32[3,96,50]{2,1,0:T(8,128)}) custom-call(bf16[3,5,48,128]{3,2,1,0:T(8,128)(2,1)} %fusion.3.pack_ref, bf16[4,192,128]{2,1,0:T(8,128)(2,1)} %pad.18.meta_ref, bf16[16,192]{1,0:T(8,128)(2,1)} %maximum_maximum_fusion.ids_ref, bf16[4,20,10]{2,1,0:T(8,128)(2,1)} %copy.47.lift_ref, bf16[10,10]{1,0:T(8,128)(2,1)} %face_ref.1, ...), custom_call_target="tpu_custom_call" | custom-call | tf_op jit(solution)/shard_map/pallas_call | solution.py:441
  38.6 1.7 %copy.48 = f32[3,96,50]{1,2,0:T(8,128)} copy(f32[3,96,50]{2,1,0:T(8,128)} %get-tuple-element.6) | data formatting | bytes 115200 | tf_op jit(solution)/shard_map/pallas_call | solution.py:441
  40.2 1.7 %copy.49 = f32[3,96,50]{1,2,0:T(8,128)} copy(f32[3,96,50]{2,1,0:T(8,128)} %get-tuple-element.7) | data formatting | bytes 115200 | tf_op jit(solution)/shard_map/pallas_call | solution.py:441
  (10 shorter events, 0.1 us)

commit v2 on v1

v2 whole, which is shorter than its diff:
```python
import functools

import jax
import jax.numpy as jnp
import numpy as np
from jax import lax
from jax.experimental import pallas as pl
from jax.experimental.pallas import tpu as pltpu
from jax.sharding import PartitionSpec as P

radau_inverse = (
    (4.325579890063155, 0.33919925181580984, 0.5417705399358749),
    (-4.178718591551905, -0.32768282076106237, 0.47662355450055044),
    (-0.5028726349457868, 2.571926949855605, -0.5960392048282249),
)
LANE = 128
HALF = 64
MESH = pl.DeviceIdType.MESH


def triangle_table(fnodes):
    degree = next(d for d in range(1, fnodes) if (d + 1) * (d + 2) // 2 == fnodes)
    lattice = [(a, b, degree - a - b) for a in range(degree + 1) for b in range(degree + 1 - a)]
    rotations = [(0, 1, 2), (1, 2, 0), (2, 0, 1), (0, 2, 1), (2, 1, 0), (1, 0, 2)]
    return [
        [lattice.index(tuple(point[corner] for corner in rotation)) for point in lattice]
        for rotation in rotations
    ]


def structure(modes, fnodes, nvar, elems, chunk):
    lane = np.arange(LANE)
    side, inside = lane // HALF, lane % HALF
    node, var = inside // nvar, inside % nvar
    used = inside < fnodes * nvar
    inner = modes * nvar
    parts, place, at = [], {}, 0

    def add(name, block):
        nonlocal at
        rows, cols = block.shape
        wide = -(-cols // LANE) * LANE
        full = np.zeros((LANE, wide), np.float32)
        full[:rows, :cols] = block
        place[name] = (at, at + wide)
        parts.append(full)
        at += wide

    row = lane[:, None]
    expand, shifts, top, bottom = [], [], [], []
    for d in range(nvar):
        other = (var + d) % nvar
        expand.append((row == (var * nvar + other)[None]) & used[None])
        shifts.append(
            (row == (side * HALF + node * nvar + other)[None]) & (used & (side == 1))[None]
        )
        fit = (row % nvar == other[None]) & used[None] & (row < inner)
        top.append(fit & (side == 0)[None])
        bottom.append(fit & (side == 1)[None])
    add("expand", np.concatenate(expand, 1))
    add("shifts", np.concatenate(shifts, 1))
    add("top", np.concatenate(top, 1))
    add("bottom", np.concatenate(bottom, 1))
    add("modes", (row // nvar == np.arange(modes)[None]) & (row < inner))
    nodes = (np.arange(fnodes)[:, None] == node[None]) & used[None]
    add("nodes", np.concatenate([nodes] * nvar, 1))
    add("rows_node", nodes.T)
    one = used & (side == 1)
    add("same", (var[:, None] == var[None]) & one[:, None] & one[None])
    table = triangle_table(fnodes)
    turns = []
    for order in table:
        order = np.array(order + [0] * HALF)
        source = side * HALF + order[node] * nvar + var
        turns.append((row == source[None]) & used[None])
    add("turns", np.concatenate(turns, 1))
    column = np.arange(chunk * inner)
    add("repeat", row == (column % inner)[None])
    third = elems // 3
    r = np.arange(elems)
    add("thirds", (3 * (r % third) + r // third)[:, None] == r[None])
    return np.concatenate(parts, 1), place, [order[1] for order in table]


def dot(a, b):
    return jnp.dot(a, b, preferred_element_type=jnp.float32)


def dot_nt(a, b):
    return lax.dot_general(a, b, (((1,), (1,)), ((), ())), preferred_element_type=jnp.float32)


def split(x):
    high = x.astype(jnp.bfloat16)
    low = (x - high.astype(jnp.float32)).astype(jnp.bfloat16)
    return jnp.concatenate([high, low], axis=0)


def kernel(
    dims,
    place,
    classes,
    inner_ref,
    face_res_ref,
    trace_ref,
    stabil_ref,
    ids_ref,
    orient_ref,
    lift_ref,
    face_ref,
    const_ref,
    factor_hbm,
    out_res,
    out_schur,
    factor,
    nodal,
    wide_in,
    stab_in,
    lift_in,
    send1,
    recv1,
    weights,
    stab,
    spread_in,
    chosen_in,
    numbers_in,
    base,
    solved,
    send2,
    recv2,
    sums,
    send3,
    recv3,
    factor_sem,
    s1,
    r1,
    s2,
    r2,
    s3,
    r3,
):
    sections, columns, elems, inner, face_size, nvar, chunk = dims
    third = elems // 3
    col_elems = sections * elems
    face_dev = 2 * elems
    col_faces = sections * face_dev
    rows = columns * 8
    f32, bf16 = jnp.float32, jnp.bfloat16
    section = lax.axis_index("section")
    column = lax.axis_index("elem")
    mine = column.astype(f32)

    def const(name):
        lo, hi = place[name]
        return const_ref[:, lo:hi]

    factor_copy = pltpu.make_async_copy(factor_hbm.at[0, 0], factor, factor_sem)
    factor_copy.start()
    barrier = pltpu.get_barrier_semaphore()
    for d in range(1, sections):
        pl.semaphore_signal(
            barrier, inc=1, device_id={"section": lax.rem(section + d, sections)}, device_id_type=MESH
        )

    def greet(d, carry):
        pl.semaphore_signal(
            barrier, inc=1, device_id={"elem": lax.rem(column + d, columns)}, device_id_type=MESH
        )
        return carry

    lax.fori_loop(1, columns, greet, 0)

    send1[...] = jnp.zeros(send1.shape, bf16)
    wide_in[...] = jnp.zeros(wide_in.shape, f32)
    thirds = const("thirds")[:elems, :elems]

    def transformed(values, g):
        row = radau_inverse[g]
        return row[0] * values[0] + row[1] * values[1] + row[2] * values[2]

    for at, source in ((0, face_res_ref), (HALF, trace_ref)):
        values = [source[t].astype(f32) for t in range(3)]
        for g in range(3):
            nodal[g] = transformed(values, g)
        for g in range(3):
            for k in range(4):
                wide_in[g, 1 + k, :, at : at + face_size] = nodal[g, :, k, :]
    values = [inner_ref[t].astype(f32) for t in range(3)]
    for g in range(3):
        wide_in[g, 0, :, :inner] = transformed(values, g)
    for g in range(3):
        for part in range(5):
            w = wide_in[g, part].astype(bf16)
            if g == 0:
                send1[0, part] = w
            else:
                w = dot(thirds, w).astype(bf16)
                for t in range(3):
                    send1[1 + t, part, (g - 1) * third : g * third] = w[t * third : (t + 1) * third]

    pl.semaphore_wait(barrier, sections - 1 + columns - 1)

    def exchange(source, target, send_sem, recv_sem):
        copies = []
        for d in range(1, sections):
            peer = lax.rem(section + d, sections)
            copy = pltpu.make_async_remote_copy(
                src_ref=source.at[peer],
                dst_ref=target.at[section],
                send_sem=send_sem.at[d],
                recv_sem=recv_sem.at[d],
                device_id={"section": peer},
                device_id_type=MESH,
            )
            copy.start()
            copies.append(copy)
        return copies

    copies1 = exchange(send1, recv1, s1, r1)
    recv1[section] = send1[section]

    lift_in[...] = lift_ref[...].astype(f32)
    stab_in[...] = stabil_ref[...].astype(f32)
    for k in range(4):
        lift_k = lift_in[:, k, :].astype(bf16)
        by_mode = dot_nt(const("modes")[:, : lift_ref.shape[2]], lift_k).astype(bf16)
        wide = dot(by_mode, const("nodes")[: lift_ref.shape[0]]).astype(bf16)
        weights[k, :LANE] = wide * const("top")
        weights[k, LANE:] = wide * const("bottom")
    rows_node = const("rows_node")[:, : face_ref.shape[0]]
    face_rows = dot(rows_node, face_ref[...]).astype(bf16)
    face_wide = (dot_nt(face_rows, rows_node) * const("same").astype(f32)).astype(bf16)
    solved[...] = jnp.zeros(solved.shape, f32)
    send3[...] = jnp.zeros(send3.shape, bf16)

    lane = lax.broadcasted_iota(jnp.int32, (1, LANE), 1)
    item = lax.broadcasted_iota(jnp.int32, (rows, 1), 0) % 8

    def prepare(count, step, offset):
        number = sections * count
        r = lax.broadcasted_iota(jnp.int32, (count, elems), 0)
        q = lax.broadcasted_iota(jnp.int32, (count, elems), 1)
        pick = jnp.where(q == step * r + offset, 1.0, 0.0).astype(bf16)
        q = lax.broadcasted_iota(jnp.int32, (elems, number), 0)
        e = lax.broadcasted_iota(jnp.int32, (elems, number), 1)
        names = jnp.zeros((16, number), f32)
        kinds = []
        for s in range(sections):
            face = ids_ref[s].astype(f32)
            strip = jnp.floor((face + 0.5) * (1.0 / face_dev))
            block = jnp.floor((strip + 0.5) * (1.0 / columns))
            slot = block * face_dev + face - strip * face_dev
            high = jnp.floor((slot + 0.5) * (1.0 / 16))
            turn = orient_ref[s, 1].astype(f32)
            table = jnp.concatenate(
                [strip - block * columns, high, slot - 16 * high, jnp.zeros_like(slot)], axis=0
            ).astype(bf16)
            put = jnp.where(q == step * (e - s * count) + offset, 1.0, 0.0).astype(bf16)
            names += dot(table, put)
            kinds.append(dot_nt(pick, turn.astype(bf16)))
        kinds = jnp.concatenate(kinds, axis=0)
        owner, slot = names[:4], 16 * names[4:8] + names[8:12]
        for k in range(4):
            per_block = [
                dot_nt(pick, stab_in[s, :, k, :].astype(bf16)) for s in range(sections)
            ]
            small = jnp.concatenate(per_block, axis=0).astype(bf16)
            stab[k, :number, : nvar * LANE] = dot(small, const("expand")[: nvar * nvar])
            stab[k, :number, nvar * LANE :] = jnp.broadcast_to(kinds[:, k : k + 1], (number, LANE))
        row_col = (lax.broadcasted_iota(jnp.int32, (rows, 1), 0) // 8).astype(f32)
        index = lax.broadcasted_iota(jnp.int32, (1, number), 1).astype(f32)
        far = float(8 * col_elems)
        least = jnp.full((rows, 1), far, f32)
        most = jnp.full((rows, 1), -1.0, f32)
        for k in range(4):
            mark = (owner[k : k + 1] == row_col) & (row_col != mine)
            at = index + k * number
            least = jnp.minimum(least, jnp.min(jnp.where(mark, at, far), 1, keepdims=True))
            most = jnp.maximum(most, jnp.max(jnp.where(mark, at, -1.0), 1, keepdims=True))
        wanted = jnp.where(item % 2 == 0, least, jnp.where(most > least, most, -1.0))
        faces = lax.broadcasted_iota(jnp.int32, (col_faces, 1), 0).astype(f32)
        numbers = jnp.zeros((rows, 1), f32)
        for k in range(4):
            local_slot = jnp.where(owner[k : k + 1] == mine, slot[k : k + 1], -1.0)
            spread_in[k, :, :number] = jnp.where(faces == local_slot, 1.0, 0.0).astype(bf16)
            chosen = jnp.where(index + k * number == wanted, 1.0, 0.0)
            numbers += jnp.sum(chosen * (slot[k : k + 1] + 1.0), 1, keepdims=True)
            chosen_in[k, :, :number] = chosen
        numbers_in[...] = jnp.broadcast_to(numbers - 1.0, (rows, LANE))

    def work(parts, count, take):
        number = sections * count
        total = parts * number
        lifted = [None] * parts
        for k in range(4):
            for c in range(parts):
                traced = take(c, 1 + k)
                shifted = dot(traced, const("shifts"))
                weighted = jnp.zeros((number, LANE), f32)
                for d in range(nvar):
                    weighted += (
                        stab[k, :number, d * LANE : (d + 1) * LANE]
                        * shifted[:, d * LANE : (d + 1) * LANE]
                    )
                pair = split(weighted)
                term = dot_nt(pair, weights[k, LANE:, :LANE])
                term = term[:number] + term[number:]
                lifted[c] = term if k == 0 else lifted[c] + term
                own = dot_nt(pair, face_wide)
                own = own[:number] + own[number:]
                base[k, c * number : (c + 1) * number] = jnp.where(
                    lane < HALF, traced.astype(f32), own
                )
        vectors = [take(c, 0) for c in range(parts)] + [x.astype(bf16) for x in lifted]
        per = len(vectors) * chunk
        begins = list(range(0, number, chunk))
        right = jnp.concatenate([x[b : b + chunk] for b in begins for x in vectors], axis=0)
        reals = [jnp.zeros((per, inner), f32) for _ in begins]
        imags = [jnp.zeros((per, inner), f32) for _ in begins]
        first, span = place["repeat"][0], chunk * inner
        for lo in range(0, span, 512):
            hi = min(lo + 512, span)
            wide = dot(right, const_ref[:, first + lo : first + hi]).astype(bf16)
            r = lax.broadcasted_iota(jnp.int32, (chunk, hi - lo), 0) * inner
            at = lax.broadcasted_iota(jnp.int32, (chunk, hi - lo), 1) + lo - r
            mask = jnp.where((at >= 0) & (at < inner), 1.0, 0.0).astype(bf16)
            wide = wide * jnp.concatenate([mask] * (right.shape[0] // chunk), axis=0)
            for n, b in enumerate(begins):
                cut = wide[n * per : (n + 1) * per]
                reals[n] += dot_nt(cut, factor[:, b * inner + lo : b * inner + hi])
                if parts == 2:
                    at = (number + b) * inner
                    imags[n] += dot_nt(cut, factor[:, at + lo : at + hi])
        for n, b in enumerate(begins):
            for side in range(2):
                lanes = slice(side * LANE, side * LANE + inner)
                one = slice(parts * side * chunk, (parts * side + 1) * chunk)
                if parts == 1:
                    solved[b : b + chunk, lanes] = reals[n][one]
                else:
                    two = slice((2 * side + 1) * chunk, (2 * side + 2) * chunk)
                    solved[b : b + chunk, lanes] = reals[n][one] - imags[n][two]
                    solved[number + b : number + b + chunk, lanes] = imags[n][one] + reals[n][two]
        both = solved[:total].astype(bf16)
        items = jnp.zeros((rows, LANE), f32)
        local = [jnp.zeros((col_faces, LANE), f32) for _ in range(parts)]
        for k in range(4):
            mixed = dot(both, weights[k])
            for c in range(parts):
                cut = slice(c * number, (c + 1) * number)
                pay = base[k, cut]
                for d in range(nvar):
                    pay -= (
                        stab[k, :number, d * LANE : (d + 1) * LANE]
                        * mixed[cut, d * LANE : (d + 1) * LANE]
                    )
                turned = dot(pay.astype(bf16), const("turns"))
                kind = stab[k, :number, nvar * LANE :]
                result = jnp.zeros((number, LANE), f32)
                for n, name in enumerate(classes):
                    result = jnp.where(
                        kind == float(name), turned[:, n * LANE : (n + 1) * LANE], result
                    )
                result = result.astype(bf16)
                local[c] += dot(spread_in[k, :, :number], result)
                picked = jnp.where(item // 2 == c, chosen_in[k, :, :number], 0.0).astype(bf16)
                items += dot(picked, result)
        numbers = jnp.where(item < 2 * parts, numbers_in[...], -1.0)
        items = jnp.where(lane == HALF - 1, numbers, items)
        send2[...] = items.reshape(columns, 8, LANE)
        for c in range(parts):
            sums[c] = local[c]
        if parts == 1:
            sums[1] = jnp.zeros((col_faces, LANE), f32)

    @pl.when(section == 0)
    def _():
        prepare(elems, 1, 0)

    @pl.when(section != 0)
    def _():
        prepare(third, 3, section - 1)

    for copy in copies1:
        copy.wait()
    factor_copy.wait()

    @pl.when(section == 0)
    def _():
        def take(c, part):
            return jnp.concatenate([recv1[s, part] for s in range(sections)], axis=0)

        work(1, elems, take)

    @pl.when(section != 0)
    def _():
        def take(c, part):
            return jnp.concatenate(
                [recv1[s, part, c * third : (c + 1) * third] for s in range(sections)], axis=0
            )

        work(2, third, take)

    def item_copy(d):
        peer = lax.rem(column + d, columns)
        return pltpu.make_async_remote_copy(
            src_ref=send2.at[peer],
            dst_ref=recv2.at[column],
            send_sem=s2.at[d],
            recv_sem=r2.at[d],
            device_id={"elem": peer},
            device_id_type=MESH,
        )

    def start_item(d, carry):
        item_copy(d).start()
        return carry

    def end_item(d, carry):
        item_copy(d).wait()
        return carry

    lax.fori_loop(1, columns, start_item, 0)
    recv2[column] = send2[column]
    lax.fori_loop(1, columns, end_item, 0)
    arrived = recv2[...].reshape(rows, LANE)
    numbers = arrived[:, HALF - 1 : HALF]
    faces = lax.broadcasted_iota(jnp.int32, (1, col_faces), 1).astype(f32)
    for c in range(2):
        hits = jnp.where((numbers == faces) & (item // 2 == c), 1.0, 0.0)
        spread = jnp.transpose(hits).astype(bf16)
        full = (sums[c] + dot(spread, arrived.astype(bf16))).astype(bf16)
        for s in range(sections):
            send3[s, c] = full[s * face_dev : (s + 1) * face_dev]

    copies3 = exchange(send3, recv3, s3, r3)
    recv3[section] = send3[section]
    for copy in copies3:
        copy.wait()
    groups = [(0, 0, 1), (0, 1, sections), (1, 1, sections)]
    for g, (part, begin, end) in enumerate(groups):
        total = recv3[begin, part].astype(f32)
        for s in range(begin + 1, end):
            total += recv3[s, part].astype(f32)
        total = jnp.transpose(total)
        out_res[g] = total[:face_size]
        out_schur[g] = total[HALF : HALF + face_size]


def on_device(
    interior_res,
    face_res,
    trace_vals,
    stabil,
    element_faces,
    orient,
    lift_matrix,
    face_matrix,
    factors,
):
    sections = lax.axis_size("section")
    columns = lax.axis_size("elem")
    elems, inner = interior_res.shape[3:]
    face_size = face_res.shape[5]
    fnodes = face_matrix.shape[0]
    modes = lift_matrix.shape[1]
    nvar = face_size // fnodes
    chunk = 32
    col_elems = sections * elems
    face_dev = 2 * elems
    col_faces = sections * face_dev
    f32, bf16 = jnp.float32, jnp.bfloat16
    consts, place, classes = structure(modes, fnodes, nvar, elems, chunk)

    dims = (sections, columns, elems, inner, face_size, nvar, chunk)
    out = jax.ShapeDtypeStruct((3, face_size, face_dev), f32)
    vmem = pl.BlockSpec(memory_space=pltpu.VMEM)
    residual, schur = pl.pallas_call(
        functools.partial(kernel, dims, place, classes),
        out_shape=(out, out),
        in_specs=[vmem] * 9 + [pl.BlockSpec(memory_space=pl.ANY)],
        out_specs=(vmem, vmem),
        scratch_shapes=[
            pltpu.VMEM(factors.shape[2:], bf16),
            pltpu.VMEM((3, elems, 4, face_size), f32),
            pltpu.VMEM((3, 5, elems, LANE), f32),
            pltpu.VMEM((sections, nvar * nvar, 4, elems), f32),
            pltpu.VMEM((fnodes, 4, modes), f32),
            pltpu.VMEM((sections, 5, elems, LANE), bf16),
            pltpu.VMEM((sections, 5, elems, LANE), bf16),
            pltpu.VMEM((4, 2 * LANE, nvar * LANE), bf16),
            pltpu.VMEM((4, col_elems, (nvar + 1) * LANE), f32),
            pltpu.VMEM((4, col_faces, col_elems), bf16),
            pltpu.VMEM((4, columns * 8, col_elems), f32),
            pltpu.VMEM((columns * 8, LANE), f32),
            pltpu.VMEM((4, col_elems, LANE), f32),
            pltpu.VMEM((col_elems, 2 * LANE), f32),
            pltpu.VMEM((columns, 8, LANE), f32),
            pltpu.VMEM((columns, 8, LANE), f32),
            pltpu.VMEM((2, col_faces, LANE), f32),
            pltpu.VMEM((sections, 2, face_dev, LANE), bf16),
            pltpu.VMEM((sections, 2, face_dev, LANE), bf16),
            pltpu.SemaphoreType.DMA,
            pltpu.SemaphoreType.DMA((sections,)),
            pltpu.SemaphoreType.DMA((sections,)),
            pltpu.SemaphoreType.DMA((columns,)),
            pltpu.SemaphoreType.DMA((columns,)),
            pltpu.SemaphoreType.DMA((sections,)),
            pltpu.SemaphoreType.DMA((sections,)),
        ],
        compiler_params=pltpu.CompilerParams(
            collective_id=0, has_side_effects=True, vmem_limit_bytes=56 * 2**20
        ),
    )(
        interior_res[:, 0, 0],
        face_res[:, 0, 0],
        trace_vals[:, 0, 0],
        stabil[0].transpose(0, 3, 2, 1),
        element_faces[0].transpose(0, 2, 1),
        orient[0].transpose(0, 3, 2, 1),
        lift_matrix.transpose(2, 0, 1),
        face_matrix,
        jnp.asarray(consts, bf16),
        factors,
    )
    return residual.transpose(0, 2, 1), schur.transpose(0, 2, 1)


def solution(mesh):
    return jax.shard_map(
        on_device,
        mesh=mesh,
        in_specs=(
            P(None, "elem", "section", None, None),
            P(None, "elem", "section", None, None, None),
            P(None, "elem", "section", None, None, None),
            P("elem", None, None, None, None),
            P("elem", None, None, None),
            P("elem", None, None, None, None),
            P(),
            P(),
            P("section", "elem", None, None),
        ),
        out_specs=(P(None, ("section", "elem"), None), P(None, ("section", "elem"), None)),
        check_vma=False,
    )
```

time: 42.4 us -> 30.4 us (0.72)
  local copies, waits for them, and re-layouts: 8.36 us -> 3.06 us
  other arithmetic: 4.46 us -> 0 us
  Pallas kernels: 28.4 us -> 26.4 us
    pallas_call x2 -> x0, local copies, waits for them, and re-layouts: 3.32 us -> none  [on_device(): pl.pallas_call(functools.partial(kernel, dims, place, classes), out_shape...]
    concatenate x3 -> x0, other arithmetic: 2.18 us -> none  [the longest x1 1.46 us: on_device(): pack = jnp.concatenate([widen(interior_res[:, 0], LANE), sides], axis=1)]
    pallas_call x1, Pallas kernels: 28.4 us -> 26.4 us  [on_device(): pl.pallas_call(functools.partial(kernel, dims, place, classes), out_shape...]
    squeeze x1 -> x0, local copies, waits for them, and re-layouts: 1.02 us -> none  [on_device(): trace_vals[:, 0, 0]]
    another operation x3 -> x0, other arithmetic: 0.73 us -> none
    pad x1 -> x0, local copies, waits for them, and re-layouts: 0.72 us -> none  [widen(): return jnp.pad(x, [(0, 0)] * (x.ndim - 1) + [(0, size - x.shape[-1])])]
    ne x1 -> x0, other arithmetic: 0.71 us -> none  [on_device(): face // face_dev % columns]
    div x1 -> x0, other arithmetic: 0.71 us -> none  [on_device(): face // face_dev % columns]
where the time goes in v2:
time: 30.4 us; the launch traced here: 30.1 us
  Pallas kernels  26.4 us (87%)
  local copies, waits for them, and re-layouts  3.06 us (10%)
  between operations  0.64 us (2%)
    pallas_call x1, Pallas kernels, on_device(): pl.pallas_call(functools.partial(kernel, dims, place, classes), out_shape...  26.4 us
    unnamed x2, local copies, waits for them, and re-layouts  3.06 us

profile of v2, /device:TPU:0, one launch (start us, length us, event | category | flops | bytes accessed | tf_op | source)
XLA Modules:
  0.0 30.1 jit_solution(2028474856563402160)
XLA Ops:
  0.6 26.4 %shard_map.113 = (f32[3,50,96]{2,1,0:T(8,128)}, f32[3,50,96]{2,1,0:T(8,128)}) custom-call(bf16[3,48,100]{2,1,0:T(8,128)(2,1)} %bitcast.21, bf16[3,48,4,50]{3,2,1,0:T(4,128)(2,1)} %bitcast.15, bf16[3,48,4,50]{3,2,1,0:T(4,128)(2,1)} %bitcast.16, bf16[4,25,4,48]{3,2,1,0:T(4,128)(2,1)} %bitcast.17, s32[4,4,48]{2,1,0:T(4,128)} %bitcast.23, ...), custom_call_target="tpu_custom_call" | custom-call | tf_op jit(solution)/shard_map/pallas_call | solution.py:478
  27.1 1.5 %copy.14 = f32[3,96,50]{1,2,0:T(8,128)} copy(f32[3,96,50]{1,2,0:T(8,128)} %bitcast.19) | data formatting | bytes 115200
  28.6 1.5 %copy.15 = f32[3,96,50]{1,2,0:T(8,128)} copy(f32[3,96,50]{1,2,0:T(8,128)} %bitcast.18) | data formatting | bytes 115200

commit v3 on v2

--- a/solution.py
+++ b/solution.py
@@ -28,7 +28,7 @@
     ]
 
 
-def structure(modes, fnodes, nvar, elems, chunk):
+def structure(modes, fnodes, nvar, chunk):
     lane = np.arange(LANE)
     side, inside = lane // HALF, lane % HALF
     node, var = inside // nvar, inside % nvar
@@ -76,9 +76,6 @@
     add("turns", np.concatenate(turns, 1))
     column = np.arange(chunk * inner)
     add("repeat", row == (column % inner)[None])
-    third = elems // 3
-    r = np.arange(elems)
-    add("thirds", (3 * (r % third) + r // third)[:, None] == r[None])
     return np.concatenate(parts, 1), place, [order[1] for order in table]
 
 
@@ -108,11 +105,11 @@
     orient_ref,
     lift_ref,
     face_ref,
+    const_hbm,
+    factor_hbm,
+    out,
+    factor,
     const_ref,
-    factor_hbm,
-    out_res,
-    out_schur,
-    factor,
     nodal,
     wide_in,
     stab_in,
@@ -132,6 +129,7 @@
     send3,
     recv3,
     factor_sem,
+    const_sem,
     s1,
     r1,
     s2,
@@ -154,6 +152,8 @@
         lo, hi = place[name]
         return const_ref[:, lo:hi]
 
+    const_copy = pltpu.make_async_copy(const_hbm, const_ref, const_sem)
+    const_copy.start()
     factor_copy = pltpu.make_async_copy(factor_hbm.at[0, 0], factor, factor_sem)
     factor_copy.start()
     barrier = pltpu.get_barrier_semaphore()
@@ -172,7 +172,9 @@
 
     send1[...] = jnp.zeros(send1.shape, bf16)
     wide_in[...] = jnp.zeros(wide_in.shape, f32)
-    thirds = const("thirds")[:elems, :elems]
+    r = lax.broadcasted_iota(jnp.int32, (elems, elems), 0)
+    q = lax.broadcasted_iota(jnp.int32, (elems, elems), 1)
+    thirds = jnp.where(q == 3 * (r % third) + r // third, 1.0, 0.0).astype(bf16)
 
     def transformed(values, g):
         row = radau_inverse[g]
@@ -218,6 +220,7 @@
 
     copies1 = exchange(send1, recv1, s1, r1)
     recv1[section] = send1[section]
+    const_copy.wait()
 
     lift_in[...] = lift_ref[...].astype(f32)
     stab_in[...] = stabil_ref[...].astype(f32)
@@ -442,9 +445,12 @@
         total = recv3[begin, part].astype(f32)
         for s in range(begin + 1, end):
             total += recv3[s, part].astype(f32)
-        total = jnp.transpose(total)
-        out_res[g] = total[:face_size]
-        out_schur[g] = total[HALF : HALF + face_size]
+        out[g] = jnp.transpose(total)
+
+
+def part_sides(face_size, both, out_res, out_schur):
+    out_res[...] = both[:, :face_size]
+    out_schur[...] = both[:, HALF : HALF + face_size]
 
 
 def on_device(
@@ -470,18 +476,19 @@
     face_dev = 2 * elems
     col_faces = sections * face_dev
     f32, bf16 = jnp.float32, jnp.bfloat16
-    consts, place, classes = structure(modes, fnodes, nvar, elems, chunk)
+    consts, place, classes = structure(modes, fnodes, nvar, chunk)
 
     dims = (sections, columns, elems, inner, face_size, nvar, chunk)
     out = jax.ShapeDtypeStruct((3, face_size, face_dev), f32)
     vmem = pl.BlockSpec(memory_space=pltpu.VMEM)
-    residual, schur = pl.pallas_call(
+    both = pl.pallas_call(
         functools.partial(kernel, dims, place, classes),
-        out_shape=(out, out),
-        in_specs=[vmem] * 9 + [pl.BlockSpec(memory_space=pl.ANY)],
-        out_specs=(vmem, vmem),
+        out_shape=jax.ShapeDtypeStruct((3, LANE, face_dev), f32),
+        in_specs=[vmem] * 8 + [pl.BlockSpec(memory_space=pl.ANY)] * 2,
+        out_specs=vmem,
         scratch_shapes=[
             pltpu.VMEM(factors.shape[2:], bf16),
+            pltpu.VMEM(consts.shape, bf16),
             pltpu.VMEM((3, elems, 4, face_size), f32),
             pltpu.VMEM((3, 5, elems, LANE), f32),
             pltpu.VMEM((sections, nvar * nvar, 4, elems), f32),
@@ -500,6 +507,7 @@
             pltpu.VMEM((2, col_faces, LANE), f32),
             pltpu.VMEM((sections, 2, face_dev, LANE), bf16),
             pltpu.VMEM((sections, 2, face_dev, LANE), bf16),
+            pltpu.SemaphoreType.DMA,
             pltpu.SemaphoreType.DMA,
             pltpu.SemaphoreType.DMA((sections,)),
             pltpu.SemaphoreType.DMA((sections,)),
@@ -523,6 +531,12 @@
         jnp.asarray(consts, bf16),
         factors,
     )
+    residual, schur = pl.pallas_call(
+        functools.partial(part_sides, face_size),
+        out_shape=(out, out),
+        in_specs=[vmem],
+        out_specs=(vmem, vmem),
+    )(both)
     return residual.transpose(0, 2, 1), schur.transpose(0, 2, 1)
 
 

time: 30.4 us -> 28.1 us (0.924)
  local copies, waits for them, and re-layouts: 3.06 us -> 0 us
  Pallas kernels: 26.4 us -> 27.3 us
    unnamed x2 -> x0, local copies, waits for them, and re-layouts: 3.06 us -> none
    pallas_call x0 -> x1, Pallas kernels: none -> 1.6 us  [on_device(): pl.pallas_call(functools.partial(part_sides, face_size), out_shape=(out,...]
    pallas_call x1, Pallas kernels: 26.4 us -> 25.7 us  [on_device(): pl.pallas_call(functools.partial(kernel, dims, place, classes), out_shape...]
where the time goes in v3:
time: 28.1 us; the launch traced here: 27.9 us
  Pallas kernels  27.3 us (97%)
  between operations  0.64 us (2%)
    pallas_call x1, Pallas kernels, on_device(): pl.pallas_call(functools.partial(kernel, dims, place, classes), out_shape...  25.7 us
    pallas_call x1, Pallas kernels, on_device(): pl.pallas_call(functools.partial(part_sides, face_size), out_shape=(out,...  1.6 us

profile of v3, /device:TPU:0, one launch (start us, length us, event | category | flops | bytes accessed | tf_op | source)
XLA Modules:
  0.0 27.9 jit_solution(1629036909327218163)
XLA Ops:
  0.6 25.7 %shard_map.113.both = f32[3,128,96]{2,1,0:T(8,128)} custom-call(bf16[3,48,100]{2,1,0:T(8,128)(2,1)} %bitcast.19, bf16[3,48,4,50]{3,2,1,0:T(4,128)(2,1)} %bitcast.15, bf16[3,48,4,50]{3,2,1,0:T(4,128)(2,1)} %bitcast.16, bf16[4,25,4,48]{3,2,1,0:T(4,128)(2,1)} %bitcast.17, s32[4,4,48]{2,1,0:T(4,128)} %bitcast.21, s32[4,10,4,48]{3,2,1,0:T(4,128)} %bitcast.18, ...), custom_call_target="tpu_custom_call" | custom-call | tf_op jit(solution)/shard_map/pallas_call | solution.py:484
  26.3 1.6 %shard_map.114 = (f32[3,50,96]{2,1,0:T(8,128)}, f32[3,50,96]{2,1,0:T(8,128)}) custom-call(f32[3,128,96]{2,1,0:T(8,128)} %shard_map.113.both), custom_call_target="tpu_custom_call" | custom-call | tf_op jit(solution)/shard_map/pallas_call | solution.py:534

commit v4 on v3

--- a/solution.py
+++ b/solution.py
@@ -125,7 +125,6 @@
     solved,
     send2,
     recv2,
-    sums,
     send3,
     recv3,
     factor_sem,
@@ -157,18 +156,19 @@
     factor_copy = pltpu.make_async_copy(factor_hbm.at[0, 0], factor, factor_sem)
     factor_copy.start()
     barrier = pltpu.get_barrier_semaphore()
-    for d in range(1, sections):
-        pl.semaphore_signal(
-            barrier, inc=1, device_id={"section": lax.rem(section + d, sections)}, device_id_type=MESH
-        )
-
-    def greet(d, carry):
-        pl.semaphore_signal(
-            barrier, inc=1, device_id={"elem": lax.rem(column + d, columns)}, device_id_type=MESH
-        )
-        return carry
-
-    lax.fori_loop(1, columns, greet, 0)
+    def device(step, d):
+        return {
+            "section": lax.rem(section + step, sections),
+            "elem": lax.rem(column + d, columns),
+        }
+
+    for step in range(sections):
+
+        def greet(d, carry):
+            pl.semaphore_signal(barrier, inc=1, device_id=device(step, d), device_id_type=MESH)
+            return carry
+
+        lax.fori_loop(int(step == 0), columns, greet, 0)
 
     send1[...] = jnp.zeros(send1.shape, bf16)
     wide_in[...] = jnp.zeros(wide_in.shape, f32)
@@ -200,7 +200,7 @@
                 for t in range(3):
                     send1[1 + t, part, (g - 1) * third : g * third] = w[t * third : (t + 1) * third]
 
-    pl.semaphore_wait(barrier, sections - 1 + columns - 1)
+    pl.semaphore_wait(barrier, sections * columns - 1)
 
     def exchange(source, target, send_sem, recv_sem):
         copies = []
@@ -372,9 +372,9 @@
         items = jnp.where(lane == HALF - 1, numbers, items)
         send2[...] = items.reshape(columns, 8, LANE)
         for c in range(parts):
-            sums[c] = local[c]
-        if parts == 1:
-            sums[1] = jnp.zeros((col_faces, LANE), f32)
+            full = local[c].astype(bf16)
+            for s in range(sections):
+                send3[s, c] = full[s * face_dev : (s + 1) * face_dev]
 
     @pl.when(section == 0)
     def _():
@@ -404,48 +404,56 @@
 
         work(2, third, take)
 
-    def item_copy(d):
-        peer = lax.rem(column + d, columns)
+    copies3 = exchange(send3, recv3, s3, r3)
+
+    def item_copy(step, d):
+        peer = device(step, d)
         return pltpu.make_async_remote_copy(
-            src_ref=send2.at[peer],
-            dst_ref=recv2.at[column],
-            send_sem=s2.at[d],
-            recv_sem=r2.at[d],
-            device_id={"elem": peer},
+            src_ref=send2.at[peer["elem"]],
+            dst_ref=recv2.at[section, column],
+            send_sem=s2.at[step * columns + d],
+            recv_sem=r2.at[step * columns + d],
+            device_id=peer,
             device_id_type=MESH,
         )
 
-    def start_item(d, carry):
-        item_copy(d).start()
-        return carry
-
-    def end_item(d, carry):
-        item_copy(d).wait()
-        return carry
-
-    lax.fori_loop(1, columns, start_item, 0)
-    recv2[column] = send2[column]
-    lax.fori_loop(1, columns, end_item, 0)
-    arrived = recv2[...].reshape(rows, LANE)
-    numbers = arrived[:, HALF - 1 : HALF]
-    faces = lax.broadcasted_iota(jnp.int32, (1, col_faces), 1).astype(f32)
-    for c in range(2):
-        hits = jnp.where((numbers == faces) & (item // 2 == c), 1.0, 0.0)
-        spread = jnp.transpose(hits).astype(bf16)
-        full = (sums[c] + dot(spread, arrived.astype(bf16))).astype(bf16)
-        for s in range(sections):
-            send3[s, c] = full[s * face_dev : (s + 1) * face_dev]
-
-    copies3 = exchange(send3, recv3, s3, r3)
+    for step in range(sections):
+
+        def start_item(d, carry):
+            item_copy(step, d).start()
+            return carry
+
+        lax.fori_loop(1, columns, start_item, 0)
     recv3[section] = send3[section]
+    for step in range(sections):
+
+        def end_item(d, carry):
+            item_copy(step, d).wait()
+            return carry
+
+        lax.fori_loop(1, columns, end_item, 0)
+
+    r = lax.broadcasted_iota(jnp.int32, (sections * rows, 1), 0)
+    own = (r % rows) // 8 == column
+    kind, origin = (r % 8) // 2, r // rows
+    arrived = jnp.where(own, 0.0, recv2[...].reshape(sections * rows, LANE))
+    numbers = jnp.where(own, -1.0, arrived[:, HALF - 1 : HALF])
+    numbers -= (section * face_dev).astype(f32)
+    arrived = jnp.transpose(arrived).astype(bf16)
+    faces = lax.broadcasted_iota(jnp.int32, (1, face_dev), 1).astype(f32)
+    groups = [(0, 0, 1), (0, 1, sections), (1, 1, sections)]
+    extra = []
+    for part, begin, end in groups:
+        meant = (kind == part) & (origin >= begin) & (origin < end)
+        hits = jnp.where((numbers == faces) & meant, 1.0, 0.0).astype(bf16)
+        extra.append(dot(arrived, hits))
     for copy in copies3:
         copy.wait()
-    groups = [(0, 0, 1), (0, 1, sections), (1, 1, sections)]
     for g, (part, begin, end) in enumerate(groups):
         total = recv3[begin, part].astype(f32)
         for s in range(begin + 1, end):
             total += recv3[s, part].astype(f32)
-        out[g] = jnp.transpose(total)
+        out[g] = jnp.transpose(total) + extra[g]
 
 
 def part_sides(face_size, both, out_res, out_schur):
@@ -503,16 +511,15 @@
             pltpu.VMEM((4, col_elems, LANE), f32),
             pltpu.VMEM((col_elems, 2 * LANE), f32),
             pltpu.VMEM((columns, 8, LANE), f32),
-            pltpu.VMEM((columns, 8, LANE), f32),
-            pltpu.VMEM((2, col_faces, LANE), f32),
+            pltpu.VMEM((sections, columns, 8, LANE), f32),
             pltpu.VMEM((sections, 2, face_dev, LANE), bf16),
             pltpu.VMEM((sections, 2, face_dev, LANE), bf16),
             pltpu.SemaphoreType.DMA,
             pltpu.SemaphoreType.DMA,
             pltpu.SemaphoreType.DMA((sections,)),
             pltpu.SemaphoreType.DMA((sections,)),
-            pltpu.SemaphoreType.DMA((columns,)),
-            pltpu.SemaphoreType.DMA((columns,)),
+            pltpu.SemaphoreType.DMA((sections * columns,)),
+            pltpu.SemaphoreType.DMA((sections * columns,)),
             pltpu.SemaphoreType.DMA((sections,)),
             pltpu.SemaphoreType.DMA((sections,)),
         ],

time: 28.1 us -> 27.6 us (0.982)
  Pallas kernels: 27.3 us -> 26.6 us
    pallas_call x1, Pallas kernels: 25.7 us -> 25 us  [on_device(): pl.pallas_call(functools.partial(kernel, dims, place, classes), out_shape...]
where the time goes in v4:
time: 27.6 us; the launch traced here: 27.3 us
  Pallas kernels  26.6 us (96%)
  between operations  0.64 us (2%)
    pallas_call x1, Pallas kernels, on_device(): pl.pallas_call(functools.partial(kernel, dims, place, classes), out_shape...  25 us
    pallas_call x1, Pallas kernels, on_device(): pl.pallas_call(functools.partial(part_sides, face_size), out_shape=(out,...  1.6 us

profile of v4, /device:TPU:0, one launch (start us, length us, event | category | flops | bytes accessed | tf_op | source)
XLA Modules:
  0.0 27.3 jit_solution(14260475883474713084)
XLA Ops:
  0.6 25.0 %shard_map.113.both = f32[3,128,96]{2,1,0:T(8,128)} custom-call(bf16[3,48,100]{2,1,0:T(8,128)(2,1)} %bitcast.19, bf16[3,48,4,50]{3,2,1,0:T(4,128)(2,1)} %bitcast.15, bf16[3,48,4,50]{3,2,1,0:T(4,128)(2,1)} %bitcast.16, bf16[4,25,4,48]{3,2,1,0:T(4,128)(2,1)} %bitcast.17, s32[4,4,48]{2,1,0:T(4,128)} %bitcast.21, s32[4,10,4,48]{3,2,1,0:T(4,128)} %bitcast.18, ...), custom_call_target="tpu_custom_call" | custom-call | tf_op jit(solution)/shard_map/pallas_call | solution.py:492
  25.7 1.6 %shard_map.114 = (f32[3,50,96]{2,1,0:T(8,128)}, f32[3,50,96]{2,1,0:T(8,128)}) custom-call(f32[3,128,96]{2,1,0:T(8,128)} %shard_map.113.both), custom_call_target="tpu_custom_call" | custom-call | tf_op jit(solution)/shard_map/pallas_call | solution.py:541
